TPU v7x, 512 devices: a whole 4x4x16 slice. The times are simulated.
512 devices in a mesh: dp: 8 (over x, z_hi), ep: 64 (over y, z_lo, core).
Axes of the slice: x: 4, y: 4, z: 16 (z_hi: 2, z_lo: 8; z = z_hi * 8 + z_lo), core: 2. Of those that a mesh axis runs over, the one named last changes fastest.
Arguments:
- trainer_weights: bfloat16 [64, 2, 1024, 2304], P('ep', None, 'dp'), may hold values from -0.125 to 0.125
- trainer_place: int32 [64], replicated, may hold values from 0 to 63, each once
- engine_place: int32 [64], replicated, may hold values from 0 to 63, each once
- tokens: bfloat16 [8192, 2048], P(('dp', 'ep')), may hold values from -6 to 6
- routes: int32 [8192, 8], P(('dp', 'ep')), may hold values from 0 to 63, all different within a row; in each aligned block of 16 rows (0 to 15, 16 to 31, ...) at most 4 rows name the same one
- gates: float32 [8192, 8], P(('dp', 'ep')), may hold values from 0.1 to 1
Outputs:
- mixed: bfloat16 [8192, 2048], P(('dp', 'ep'))
- slot_load: float32 [8, 64], P('dp', 'ep')
Inputs may be any that keep to these rules, and one draw needn't show every extreme that they name: `trainer_place`: a permutation of 0 to 63. `engine_place`: a permutation of 0 to 63. `routes`: the 8 experts of a row differ; among the 16 rows of one device (aligned blocks of 16 rows) no expert is named by more than 4 rows, a bound that some block reaches.
All inputs are finite; a program needn't handle non-finite values.
Results may differ from a plain program's by a relative error of at most 0.0057.
Values may be sent and summed in bfloat16 or wider, within the bound.
A program may use at most 64 MiB of HBM per device.

v0:
```python
import jax
import jax.numpy as jnp
from jax import lax
from jax.sharding import PartitionSpec as P


def reorder_columns(values, sizes, order):
    shaped = values.reshape((values.shape[0],) + sizes)
    return shaped.transpose((0,) + order).reshape(values.shape)


def on_device(trainer_weights, trainer_place, engine_place, tokens, routes, gates):
    count_ep = lax.axis_size("ep")
    count_dp = lax.axis_size("dp")
    experts = trainer_place.shape[0]
    tok_rows, fanout = routes.shape
    model_width = tokens.shape[1]
    wide = trainer_weights.shape[3]
    hidden_width = wide // 3
    piece_rows = trainer_weights.shape[2]
    share = piece_rows // count_ep
    capacity = 2 * tok_rows * fanout // count_ep
    slot_total = count_ep * capacity
    expert_ids = jnp.arange(experts, dtype=jnp.int32)
    engine_pos = jnp.argmax(engine_place[None, :] == expert_ids[:, None], axis=1)
    source_slot = jnp.argmax(trainer_place[None, :] == engine_place[:, None], axis=1)
    local = trainer_weights[0].reshape(2, count_ep, share, wide)
    spread = lax.all_to_all(local, "ep", split_axis=1, concat_axis=0, tiled=True)
    by_slot = (
        spread.reshape(count_ep // 2, 2, 2, share, wide)
        .transpose(0, 2, 1, 3, 4)
        .reshape(experts, 2 * share, wide)
    )
    ordered = jnp.take(by_slot, source_slot, axis=0)
    sizes = (2, count_dp, count_ep, share)
    order = (3, 2, 1, 4)
    back_sizes = (count_ep, count_dp, 2, share)
    back_order = (3, 2, 1, 4)
    placed_tokens = reorder_columns(tokens, sizes, order)
    flat_expert = routes.reshape(-1)
    onehot = (flat_expert[:, None] == expert_ids[None, :]).astype(jnp.int32)
    before = jnp.cumsum(onehot, axis=0) - onehot
    rank_in = jnp.sum(before * onehot, axis=1)
    target = jnp.sum(onehot * engine_pos[None, :], axis=1)
    slot_index = target * capacity + rank_in
    placing = (slot_index[None, :] == jnp.arange(slot_total, dtype=jnp.int32)[:, None]).astype(
        jnp.bfloat16
    )
    repeated = jnp.repeat(placed_tokens, fanout, axis=0)
    send_rows = jnp.dot(placing, repeated, preferred_element_type=jnp.float32).astype(jnp.bfloat16)
    target_onehot = (target[:, None] == jnp.arange(count_ep, dtype=jnp.int32)[None, :]).astype(
        jnp.int32
    )
    send_counts = jnp.sum(target_onehot, axis=0)
    received, recv_counts = (
        lax.all_to_all(send_rows, "ep", split_axis=0, concat_axis=0, tiled=True),
        lax.all_to_all(send_counts, "ep", split_axis=0, concat_axis=0, tiled=True),
    )
    slot_load = (jnp.sum(recv_counts).astype(jnp.float32) / (tok_rows * fanout)).reshape(1, 1)
    stacked = lax.all_gather(ordered[:, None], "dp", axis=1, tiled=True)
    resident = lax.all_to_all(stacked, "ep", split_axis=0, concat_axis=0, tiled=True).reshape(
        model_width, wide
    )
    both = jnp.dot(received, resident[:, : 2 * hidden_width], preferred_element_type=jnp.float32)
    hidden = (jax.nn.silu(both[:, :hidden_width]) * both[:, hidden_width:]).astype(jnp.bfloat16)
    expert_out = lax.dot_general(
        hidden,
        resident[:, 2 * hidden_width :],
        (((1,), (1,)), ((), ())),
        preferred_element_type=jnp.float32,
    ).astype(jnp.bfloat16)
    combined = lax.all_to_all(expert_out, "ep", split_axis=0, concat_axis=0, tiled=True)
    picked = combined[slot_index]
    weighted = picked.astype(jnp.float32) * gates.reshape(-1)[:, None]
    summed = jnp.sum(weighted.reshape(tok_rows, fanout, model_width), axis=1)
    mixed = reorder_columns(summed, back_sizes, back_order).astype(jnp.bfloat16)
    return (mixed, slot_load)


def solution(mesh):
    in_specs = (
        P("ep", None, "dp", None),
        P(),
        P(),
        P(("dp", "ep"), None),
        P(("dp", "ep"), None),
        P(("dp", "ep"), None),
    )
    out_specs = (P(("dp", "ep"), None), P("dp", "ep"))
    return jax.shard_map(
        on_device, mesh=mesh, in_specs=in_specs, out_specs=out_specs, check_vma=False
    )
```

profile of v0, /device:TPU:1, one launch (start us, length us, event | category | flops | bytes accessed | tf_op | source)
XLA Modules:
  0.0 997.5 jit_solution(16650364290098837150)
XLA Ops:
  7.2 2.8 reshape_squeeze.3
  10.0 1.8 copy.46
  11.8 17.3 %all-to-all-start.1 = ((bf16[2,64,2,2304]{3,2,0,1:T(2,128)(2,1)}), bf16[2,64,2,2304]{3,2,0,1:T(2,128)(2,1)S(1)}, u32[]{:S(2)}, u32[]{:S(2)}) async-start(bf16[2,64,2,2304]{3,2,0,1:T(2,128)(2,1)} %copy.46), calls=%async_computation.1 | async-start | bytes 2359296 | tf_op jit(solution)/shard_map/all_to_all | solution.py:28
  29.2 0.7 iota_reduce_fusion
  30.0 55.9 %all-to-all-done.1 = bf16[2,64,2,2304]{3,2,0,1:T(2,128)(2,1)S(1)} async-done(((bf16[2,64,2,2304]{3,2,0,1:T(2,128)(2,1)}), bf16[2,64,2,2304]{3,2,0,1:T(2,128)(2,1)S(1)}, u32[]{:S(2)}, u32[]{:S(2)}) %all-to-all-start.1) | async-done | bytes 1179680 | tf_op jit(solution)/shard_map/all_to_all | solution.py:28
  85.8 0.8 copy.56
  87.2 1.6 gather_fusion
  89.4 1.1 copy.49
  93.0 1.2 all_to_all.36
  94.3 8.4 all-to-all-start
  102.7 326.0 %all-gather.2.cloned.1.call-done = bf16[64,8,4,2304]{3,0,2,1:T(8,128)(2,1)} async-done(((bf16[64,1,4,2304]{3,0,2,1:T(8,128)(2,1)}), bf16[64,8,4,2304]{3,0,2,1:T(8,128)(2,1)}) %all-gather.2.cloned.1.call-update) | async-done | bytes 9437200 | tf_op jit(solution)/shard_map/all_gather | solution.py:60
  428.7 13.4 %copy.50 = bf16[64,8,4,2304]{3,2,1,0:T(4,128)(2,1)} copy(bf16[64,8,4,2304]{3,0,2,1:T(8,128)(2,1)} %all-gather.2.cloned.1.call-done) | data formatting | bytes 18874368 | tf_op jit(solution)/shard_map/all_gather | solution.py:60
  442.1 36.6 %all-to-all-start.2 = ((bf16[64,8,4,2304]{3,2,1,0:T(4,128)(2,1)}), bf16[64,8,4,2304]{3,2,1,0:T(4,128)(2,1)}, u32[]{:S(2)}, u32[]{:S(2)}) async-start(bf16[64,8,4,2304]{3,2,1,0:T(4,128)(2,1)} %copy.50), calls=%async_computation.2 | async-start | bytes 18874368 | tf_op jit(solution)/shard_map/all_to_all | solution.py:61
  478.8 0.7 copy.54
  479.8 411.0 %all-to-all-done.2 = bf16[64,8,4,2304]{3,2,1,0:T(4,128)(2,1)} async-done(((bf16[64,8,4,2304]{3,2,1,0:T(4,128)(2,1)}), bf16[64,8,4,2304]{3,2,1,0:T(4,128)(2,1)}, u32[]{:S(2)}, u32[]{:S(2)}) %all-to-all-start.2) | async-done | bytes 9437216 | tf_op jit(solution)/shard_map/all_to_all | solution.py:61
  890.8 7.0 all-to-all-start.4
  897.8 15.4 %reshape.101 = bf16[2048,2304]{1,0:T(8,128)(2,1)} reshape(bf16[64,8,4,2304]{3,2,1,0:T(4,128)(2,1)} %all-to-all-done.2) | data formatting | bytes 18874368 | tf_op jit(solution)/shard_map/reshape | solution.py:61
  913.2 4.6 fusion
  917.7 2.9 fusion.4
  920.7 1.2 all_to_all.43
  921.9 13.1 %all-to-all-start.3 = ((bf16[64,4,2048]{2,1,0:T(4,128)(2,1)}), bf16[64,4,2048]{2,1,0:T(4,128)(2,1)S(1)}, u32[]{:S(2)}, u32[]{:S(2)}) async-start(bf16[64,4,2048]{2,1,0:T(4,128)(2,1)} %all_to_all.43), calls=%async_computation.3 | async-start | bytes 2097152 | tf_op jit(solution)/shard_map/all_to_all | solution.py:72
  936.4 49.9 %all-to-all-done.3 = bf16[64,4,2048]{2,1,0:T(4,128)(2,1)S(1)} async-done(((bf16[64,4,2048]{2,1,0:T(4,128)(2,1)}), bf16[64,4,2048]{2,1,0:T(4,128)(2,1)S(1)}, u32[]{:S(2)}, u32[]{:S(2)}) %all-to-all-start.3) | async-done | bytes 1048608 | tf_op jit(solution)/shard_map/all_to_all | solution.py:72
  986.6 0.9 gather_fusion.1
  988.7 0.8 copy.55
  (39 shorter events, 6.3 us)
Async XLA Ops:
  11.8 17.4 %copy-start.3 = (s32[64]{0:T(128)S(1)}, s32[64]{0:T(128)}, u32[]{:S(2)}) copy-start(s32[64]{0:T(128)} %param.7) | copy-start | bytes 772
  11.8 17.4 %copy-start.4 = (s32[64]{0:T(128)S(1)}, s32[64]{0:T(128)}, u32[]{:S(2)}) copy-start(s32[64]{0:T(128)} %param.8) | copy-start | bytes 772
  11.8 74.0 %all-to-all-start.1 = ((bf16[2,64,2,2304]{3,2,0,1:T(2,128)(2,1)}), bf16[2,64,2,2304]{3,2,0,1:T(2,128)(2,1)S(1)}, u32[]{:S(2)}, u32[]{:S(2)}) async-start(bf16[2,64,2,2304]{3,2,0,1:T(2,128)(2,1)} %copy.46), calls=%async_computation.1 | async-start | bytes 2359296 | tf_op jit(solution)/shard_map/all_to_all | solution.py:28
  29.2 399.5 %all-gather.2.cloned.1.call-start = ((), (), s32[]{:S(2)}) async-start(), calls=%async_computation.5 | async-start | bytes 10616832 | tf_op jit(solution)/shard_map/all_gather | solution.py:60
  89.3 1.2 copy-start
  90.5 0.9 copy-start.1
  94.3 347.8 %all-to-all-start = ((bf16[64,4,2048]{2,1,0:T(4,128)(2,1)}), bf16[64,4,2048]{2,1,0:T(4,128)(2,1)S(1)}, u32[]{:S(2)}, u32[]{:S(2)}) async-start(bf16[64,4,2048]{2,1,0:T(4,128)(2,1)} %all_to_all.36), calls=%async_computation | async-start | bytes 2097152 | tf_op jit(solution)/shard_map/all_to_all | solution.py:56
  442.1 448.7 %all-to-all-start.2 = ((bf16[64,8,4,2304]{3,2,1,0:T(4,128)(2,1)}), bf16[64,8,4,2304]{3,2,1,0:T(4,128)(2,1)}, u32[]{:S(2)}, u32[]{:S(2)}) async-start(bf16[64,8,4,2304]{3,2,1,0:T(4,128)(2,1)} %copy.50), calls=%async_computation.2 | async-start | bytes 18874368 | tf_op jit(solution)/shard_map/all_to_all | solution.py:61
  890.8 31.1 %all-to-all-start.4 = ((s32[64,1,1]{2,1,0:T(1,128)}), s32[64,1,1]{2,1,0:T(1,128)S(1)}, u32[]{:S(2)}, u32[]{:S(2)}) async-start(s32[64,1,1]{2,1,0:T(1,128)} %copy.54), calls=%async_computation.4 | async-start | bytes 65536 | tf_op jit(solution)/shard_map/all_to_all | solution.py:57
  920.7 14.3 %copy-start.2 = (f32[16,8]{0,1:T(8,128)S(1)}, f32[16,8]{0,1:T(8,128)}, u32[]{:S(2)}) copy-start(f32[16,8]{0,1:T(8,128)} %param.11) | copy-start | bytes 1540
  921.9 64.4 %all-to-all-start.3 = ((bf16[64,4,2048]{2,1,0:T(4,128)(2,1)}), bf16[64,4,2048]{2,1,0:T(4,128)(2,1)S(1)}, u32[]{:S(2)}, u32[]{:S(2)}) async-start(bf16[64,4,2048]{2,1,0:T(4,128)(2,1)} %all_to_all.43), calls=%async_computation.3 | async-start | bytes 2097152 | tf_op jit(solution)/shard_map/all_to_all | solution.py:72
Sparse Core Ops, SparseCore 0:
  90.6 338.0 all-gather.1
where the time goes:
time: 999 us; the launch traced here: 998 us
  waiting for transfers between devices  843 us (84%)
  starting transfers between devices  82.4 us (8%)
  local copies, waits for them, and re-layouts  44.7 us (4%)
  between operations  16 us (2%)
    all_to_all x1, waiting for transfers between devices, on_device(): lax.all_to_all(stacked, 'ep', split_axis=0, concat_axis=0, tiled=True)  411 us
    all_gather x1, waiting for transfers between devices, on_device(): stacked = lax.all_gather(ordered[:, None], 'dp', axis=1, tiled=True)  326 us
    all_to_all x1, waiting for transfers between devices, on_device(): lax.all_to_all(local, 'ep', split_axis=1, concat_axis=0, tiled=True)  55.9 us
    all_to_all x1, waiting for transfers between devices, on_device(): lax.all_to_all(expert_out, 'ep', split_axis=0, concat_axis=0, tiled=True)  49.9 us
    all_to_all x1, starting transfers between devices, on_device(): lax.all_to_all(stacked, 'ep', split_axis=0, concat_axis=0, tiled=True)  36.6 us
  transfers between devices with their start and end apart: 6, of which 4 were waited for; matrix products, arithmetic and copies ran while one was open for 4% of the time, Pallas kernels for 0%

commit v1 on v0

v1 whole, which is shorter than its diff:
```python
import functools

import jax
import jax.numpy as jnp
from jax import lax
from jax.experimental import pallas as pl
from jax.experimental.pallas import tpu as pltpu
from jax.sharding import PartitionSpec as P

MESH = pl.DeviceIdType.MESH
NX, NY, NZ = 4, 4, 16
ZLO = 8
D = 2048
FF = 768
HALF = FF // 2
ROWS = 16
TOP = 8
CAP = 4
PIECE = 128
COL = NZ * ROWS
SEND = NZ * CAP
CHUNKS = 2
WIDTH = D // CHUNKS
STEPS = NZ // 2
BF16, F32 = jnp.bfloat16, jnp.float32


def device(x, y, z, core):
    return (x * 2 + z // ZLO, (y * ZLO + z % ZLO) * 2 + core)


def layer_kernel(
    place_ref, engine_ref, weights, tokens_ref, routes_ref, gates_ref,
    mixed_ref, load_ref,
    matrix, token_all, meta_all, rows_out, rows_all, pick_hi, pick_lo, hidden,
    cross_out, cross_in, own_sum, back_out, back_in, mixing, ring_out, ring_in,
    hist_out, hist_in,
    local_sem, send_sem, matrix_sem, token_sem, meta_sem, rows_sem, twin_sem,
    cross_sem, back_sem, ring_sem, hist_sem,
):
    dp, ep = lax.axis_index("dp"), lax.axis_index("ep")
    x, z_hi = dp // 2, dp % 2
    y, z_lo, core = ep // 16, (ep // 2) % ZLO, ep % 2
    z = z_hi * ZLO + z_lo
    far = (z + ZLO) % NZ
    z_other = 1 - z_hi
    twin = 1 - core

    token_all[z] = tokens_ref[...]
    own_meta = jnp.zeros((ROWS, 128), F32)
    meta_all[z] = own_meta
    meta_all[z, :, 0:TOP] = routes_ref[...].astype(F32)
    meta_all[z, :, TOP:2 * TOP] = gates_ref[...]

    partners = []
    for k in range(NX):
        for other in (core, twin):
            if not (k == 0 and other is core):
                partners.append(device((x + k) % NX, y, z, other))
    for k in range(1, NY):
        for other in (core, twin):
            partners.append(device(x, (y + k) % NY, z, other))
    for other in (core, twin):
        partners.append(device(x, y, far, other))
    right = device(x, y, (z + 1) % NZ, core)
    left = device(x, y, (z + NZ - 1) % NZ, core)
    partners += [right, left]
    barrier = pltpu.get_barrier_semaphore()
    for partner in partners:
        pl.semaphore_signal(barrier, inc=1, device_id=partner, device_id_type=MESH)
    pl.semaphore_wait(barrier, len(partners))

    sends = []

    def send(src, dst, sem, to):
        copy = pltpu.make_async_remote_copy(
            src_ref=src, dst_ref=dst, send_sem=send_sem.at[len(sends)], recv_sem=sem,
            device_id=to, device_id_type=MESH,
        )
        copy.start()
        sends.append(copy)

    def arrived(ref, sem):
        pltpu.make_async_copy(ref, ref, sem).wait()

    def piece(part, core_of, dp_of):
        return matrix.at[part, pl.ds(pl.multiple_of(core_of * 1024 + dp_of * PIECE, PIECE), PIECE)]

    def own_piece(slot, part, half):
        return weights.at[slot, :, pl.ds(pl.multiple_of(part * FF + half * HALF, 128), HALF)]

    def piece_arrived(part, core_of, dp_of):
        arrived(piece(part, core_of, dp_of), matrix_sem.at[part, core_of * 8 + dp_of])

    def cross_part(part):
        for half in (core, twin):
            send(own_piece(z_other, part, half), piece(part, core, dp),
                 matrix_sem.at[part, core * 8 + dp], device(x, y, far, half))

    locals_ = []

    def spread_part(part):
        copy = pltpu.make_async_copy(own_piece(z_hi, part, core), piece(part, core, dp), local_sem.at[part])
        copy.start()
        locals_.append(copy)
        for half in (core, twin):
            for k in (1, 3, 2, 0):
                if k == 0 and half is core:
                    continue
                send(own_piece(z_hi, part, half), piece(part, core, dp),
                     matrix_sem.at[part, core * 8 + dp], device((x + k) % NX, y, z, half))

    def relay_part(part):
        dp_far = x * 2 + z_other
        for core_of in (core, twin):
            piece_arrived(part, core_of, dp_far)
            for k in (1, 3, 2):
                send(piece(part, core_of, dp_far), piece(part, core_of, dp_far),
                     matrix_sem.at[part, core_of * 8 + dp_far], device((x + k) % NX, y, z, core))

    def part_arrived(part):
        locals_[part].wait()
        for k in range(NX):
            for core_of in (core, twin):
                if not (k == 0 and core_of is core):
                    piece_arrived(part, core_of, ((x + k) % NX) * 2 + z_hi)
                if k > 0:
                    piece_arrived(part, core_of, ((x + k) % NX) * 2 + z_other)

    def token_view(block, step, way):
        if step == STEPS:
            return token_all.at[block, :, pl.ds(way * (D // 2), D // 2)]
        return token_all.at[block]

    def token_send(step):
        block = (z + NZ - step + 1) % NZ
        send(token_view(block, step, 0), token_view(block, step, 0), token_sem.at[0, step - 1], right)
        send(meta_all.at[block], meta_all.at[block], meta_sem.at[0, step - 1], right)
        block = (z + step - 1) % NZ
        send(token_view(block, step, 1), token_view(block, step, 1), token_sem.at[1, step - 1], left)
        if step < STEPS:
            send(meta_all.at[block], meta_all.at[block], meta_sem.at[1, step - 1], left)

    def token_arrived(step):
        block = (z + NZ - step) % NZ
        arrived(token_view(block, step, 0), token_sem.at[0, step - 1])
        arrived(meta_all.at[block], meta_sem.at[0, step - 1])
        block = (z + step) % NZ
        arrived(token_view(block, step, 1), token_sem.at[1, step - 1])
        if step < STEPS:
            arrived(meta_all.at[block], meta_sem.at[1, step - 1])

    token_send(1)
    for part in range(3):
        cross_part(part)
    for part in range(3):
        spread_part(part)
    for step in range(1, STEPS + 1):
        token_arrived(step)
        if step < STEPS:
            token_send(step + 1)
        if step == STEPS // 2:
            relay_part(0)

    turned = meta_all[...].reshape(COL, 128).T
    chosen, gate = turned[0:TOP], turned[TOP:2 * TOP]
    expert_row = lax.broadcasted_iota(jnp.int32, (64, COL), 0).astype(F32)
    lane64 = lax.broadcasted_iota(jnp.int32, (64, COL), 1)
    named = jnp.zeros((64, COL), F32)
    for k in range(TOP):
        named = named + jnp.where(chosen[k:k + 1] == expert_row, 1.0, 0.0)
    ours = jnp.where(
        lax.broadcasted_iota(jnp.int32, (8, COL), 1) // (COL // 2) == z_hi, 1.0, 0.0)
    hist_out[...] = lax.dot_general(
        ours, jnp.concatenate([named, jnp.zeros((64, COL), F32)], axis=0),
        (((1,), (1,)), ((), ())), preferred_element_type=F32)
    hist_in[0] = hist_out[...]
    for k in range(NY):
        for index, other in enumerate((core, twin)):
            if k + index > 0:
                send(hist_out, hist_in.at[2 * k + index], hist_sem.at[2 * k + index],
                     device(x, (y + k) % NY, z, other))

    row8 = lax.broadcasted_iota(jnp.int32, (8, COL), 0)
    match = jnp.zeros((8, COL), F32)
    hits, weight = [], []
    for k in range(NY):
        wanted = place_ref[2 * (((y + k) % NY) * ZLO + z_lo) + z_hi].astype(F32)
        same = jnp.where(chosen == wanted, 1.0, 0.0)
        hits.append(jnp.sum(same, axis=0, keepdims=True))
        weight.append(jnp.sum(same * gate, axis=0, keepdims=True))
        match = match + jnp.where(row8 == k, hits[k], 0.0)
    before = lax.broadcasted_iota(jnp.int32, (COL, COL), 0)
    after = lax.broadcasted_iota(jnp.int32, (COL, COL), 1)
    earlier = jnp.where((before < after) & (before // ROWS == after // ROWS), 1.0, 0.0).astype(BF16)
    rank = jnp.dot(match.astype(BF16), earlier, preferred_element_type=F32)
    sent_row = lax.broadcasted_iota(jnp.int32, (SEND, COL), 0)
    sent_rank = (sent_row % CAP).astype(F32)
    same_block = sent_row // CAP == lane64 // ROWS
    picks = []
    for k in range(NY):
        picks.append(jnp.where(same_block & (sent_rank == rank[k:k + 1]), hits[k], 0.0))
    pick = jnp.concatenate(picks, axis=0)
    scaled = jnp.concatenate([picks[k] * weight[k] for k in range(NY)], axis=0).T
    high = scaled.astype(BF16)
    pick_hi[...] = high
    pick_lo[...] = (scaled - high.astype(F32)).astype(BF16)
    pick = pick.astype(BF16)
    every = token_all[...].reshape(COL, D)
    for k in (2, 1, 3, 0):
        moved = jnp.dot(pick[k * SEND:(k + 1) * SEND], every, preferred_element_type=F32).astype(BF16)
        if k == 0:
            rows_all[core, y] = moved
            send(rows_all.at[core, y], rows_all.at[core, y], twin_sem.at[0], device(x, y, z, twin))
        else:
            rows_out[k - 1] = moved
            send(rows_out.at[k - 1], rows_all.at[core, y], rows_sem.at[k], device(x, (y + k) % NY, z, core))
    relay_part(1)
    for k in (1, 3, 2):
        giver = (y + NY - k) % NY
        arrived(rows_all.at[core, giver], rows_sem.at[k])
        send(rows_all.at[core, giver], rows_all.at[core, giver], twin_sem.at[k], device(x, y, z, twin))
    for k in range(NY):
        arrived(rows_all.at[twin, (y + NY - k) % NY], twin_sem.at[k])

    part_arrived(0)
    part_arrived(1)
    for plane in range(2):
        rows = rows_all[plane].reshape(NY * SEND, D)
        a = jnp.dot(rows, matrix[0], preferred_element_type=F32)
        b = jnp.dot(rows, matrix[1], preferred_element_type=F32)
        hidden[plane] = (a / (1.0 + jnp.exp(-a)) * b).astype(BF16)
    relay_part(2)
    part_arrived(2)

    def cols(chunk):
        return pl.ds(chunk * WIDTH, WIDTH)

    nt = (((1,), (1,)), ((), ()))
    for chunk in range(CHUNKS):
        down = matrix[2, cols(chunk)]
        cross_out[chunk] = lax.dot_general(hidden[twin], down, nt, preferred_element_type=F32).astype(BF16)
        send(cross_out.at[chunk], cross_in.at[chunk], cross_sem.at[chunk], device(x, y, z, twin))
    for chunk in range(CHUNKS):
        down = matrix[2, cols(chunk)]
        own_sum[chunk] = lax.dot_general(hidden[core], down, nt, preferred_element_type=F32)
    for chunk in range(CHUNKS):
        arrived(cross_in.at[chunk], cross_sem.at[chunk])
        total = (own_sum[chunk] + cross_in[chunk].astype(F32)).astype(BF16)
        back_out[chunk] = total.reshape(NY, SEND, WIDTH)
        for k in (2, 1, 3):
            giver = (y + NY - k) % NY
            send(back_out.at[chunk, giver], back_in.at[chunk, k], back_sem.at[chunk, k], device(x, giver, z, core))
        back_in[chunk, 0] = back_out[chunk, y]

    def ring_send(step, chunk):
        send(ring_out.at[0, step - 1, chunk], ring_in.at[0, step - 1, chunk], ring_sem.at[0, step - 1, chunk], right)
        if step < STEPS:
            send(ring_out.at[1, step - 1, chunk], ring_in.at[1, step - 1, chunk], ring_sem.at[1, step - 1, chunk], left)

    for chunk in range(CHUNKS):
        for k in (1, 3, 2):
            arrived(back_in.at[chunk, k], back_sem.at[chunk, k])
        got = back_in[chunk].reshape(NY * SEND, WIDTH)
        total = jnp.dot(pick_hi[...], got, preferred_element_type=F32)
        total = total + jnp.dot(pick_lo[...], got, preferred_element_type=F32)
        mixing[chunk] = total.reshape(NZ, ROWS, WIDTH)
        ring_out[0, 0, chunk] = mixing[chunk, (z + STEPS) % NZ].astype(BF16)
        ring_out[1, 0, chunk] = mixing[chunk, (z + NZ - STEPS + 1) % NZ].astype(BF16)
        ring_send(1, chunk)
    for step in range(1, STEPS):
        for chunk in range(CHUNKS):
            arrived(ring_in.at[0, step - 1, chunk], ring_sem.at[0, step - 1, chunk])
            block = mixing[chunk, (z + STEPS - step) % NZ] + ring_in[0, step - 1, chunk].astype(F32)
            ring_out[0, step, chunk] = block.astype(BF16)
            if step < STEPS - 1:
                arrived(ring_in.at[1, step - 1, chunk], ring_sem.at[1, step - 1, chunk])
                block = mixing[chunk, (z + NZ - STEPS + 1 + step) % NZ] + ring_in[1, step - 1, chunk].astype(F32)
                ring_out[1, step, chunk] = block.astype(BF16)
            if step < STEPS - 1:
                ring_send(step + 1, chunk)
            else:
                send(ring_out.at[0, step, chunk], ring_in.at[0, step, chunk], ring_sem.at[0, step, chunk], right)
    for chunk in range(CHUNKS):
        arrived(ring_in.at[1, STEPS - 2, chunk], ring_sem.at[1, STEPS - 2, chunk])
        arrived(ring_in.at[0, STEPS - 1, chunk], ring_sem.at[0, STEPS - 1, chunk])
        block = mixing[chunk, z] + ring_in[0, STEPS - 1, chunk].astype(F32) + ring_in[1, STEPS - 2, chunk].astype(F32)
        mixed_ref[:, cols(chunk)] = block.astype(BF16)

    for index in range(1, 2 * NY):
        arrived(hist_in.at[index], hist_sem.at[index])
    counts = jnp.sum(hist_in[...], axis=0)
    lane = lax.broadcasted_iota(jnp.int32, (8, 128), 1)
    mine = jnp.sum(jnp.where(lane == engine_ref[ep], counts, 0.0), axis=1, keepdims=True)
    load_ref[...] = mine[0:1] / (ROWS * TOP)
    for copy in sends:
        copy.wait_send()


def on_device(trainer_weights, trainer_place, engine_place, tokens, routes, gates):
    smem = pl.BlockSpec(memory_space=pltpu.SMEM)
    vmem = pl.BlockSpec(memory_space=pltpu.VMEM)
    dma = pltpu.SemaphoreType.DMA
    return pl.pallas_call(
        layer_kernel,
        out_shape=(
            jax.ShapeDtypeStruct((ROWS, D), BF16),
            jax.ShapeDtypeStruct((1, 1), F32),
        ),
        in_specs=[smem, smem, pl.BlockSpec(memory_space=pl.ANY), vmem, vmem, vmem],
        out_specs=(vmem, vmem),
        scratch_shapes=[
            pltpu.VMEM((3, D, HALF), BF16),
            pltpu.VMEM((NZ, ROWS, D), BF16),
            pltpu.VMEM((NZ, ROWS, 128), F32),
            pltpu.VMEM((NY - 1, SEND, D), BF16),
            pltpu.VMEM((2, NY, SEND, D), BF16),
            pltpu.VMEM((COL, NY * SEND), BF16),
            pltpu.VMEM((COL, NY * SEND), BF16),
            pltpu.VMEM((2, NY * SEND, HALF), BF16),
            pltpu.VMEM((CHUNKS, NY * SEND, WIDTH), BF16),
            pltpu.VMEM((CHUNKS, NY * SEND, WIDTH), BF16),
            pltpu.VMEM((CHUNKS, NY * SEND, WIDTH), F32),
            pltpu.VMEM((CHUNKS, NY, SEND, WIDTH), BF16),
            pltpu.VMEM((CHUNKS, NY, SEND, WIDTH), BF16),
            pltpu.VMEM((CHUNKS, NZ, ROWS, WIDTH), F32),
            pltpu.VMEM((2, STEPS, CHUNKS, ROWS, WIDTH), BF16),
            pltpu.VMEM((2, STEPS, CHUNKS, ROWS, WIDTH), BF16),
            pltpu.VMEM((8, 128), F32),
            pltpu.VMEM((2 * NY, 8, 128), F32),
            dma((3,)),
            dma((160,)),
            dma((3, 16)),
            dma((2, STEPS)),
            dma((2, STEPS)),
            dma((NY,)),
            dma((NY,)),
            dma((CHUNKS,)),
            dma((CHUNKS, NY)),
            dma((2, STEPS, CHUNKS)),
            dma((2 * NY,)),
        ],
        compiler_params=pltpu.CompilerParams(
            collective_id=0, has_side_effects=True, vmem_limit_bytes=48 * 2**20
        ),
    )(trainer_place, engine_place, trainer_weights[0], tokens, routes, gates)


def solution(mesh):
    in_specs = (
        P("ep", None, "dp", None),
        P(),
        P(),
        P(("dp", "ep"), None),
        P(("dp", "ep"), None),
        P(("dp", "ep"), None),
    )
    out_specs = (P(("dp", "ep"), None), P("dp", "ep"))
    return jax.shard_map(
        on_device, mesh=mesh, in_specs=in_specs, out_specs=out_specs, check_vma=False
    )
```

time: 999 us -> 179 us (0.18)
  the two profiles are of different devices: /device:TPU:1 before, /device:TPU:32 now
where the time goes in v1:
time: 179 us; the launch traced here: 178 us
  Pallas kernels  170 us (95%)
  local copies, waits for them, and re-layouts  5.57 us (3%)
  between operations  2.39 us (1%)
    pallas_call x1, Pallas kernels, on_device(): pl.pallas_call(layer_kernel, out_shape=(jax.ShapeDtypeStruct((ROWS, D), B...  170 us
    unnamed x11, local copies, waits for them, and re-layouts  5.57 us

profile of v1, /device:TPU:32, one launch (start us, length us, event | category | flops | bytes accessed | tf_op | source)
XLA Modules:
  0.0 178.4 jit_solution(191922859806871779)
XLA Ops:
  0.6 0.8 copy.8.routes_ref
  1.4 0.8 copy.9.gates_ref
  2.1 0.0 copy-start
  2.1 1.3 copy-done
  3.4 0.0 copy-start.1
  3.4 0.8 copy-done.1
  4.3 0.0 copy-start.2
  4.3 0.7 copy-done.2
  4.9 0.0 copy-start.3
  4.9 0.7 copy-done.3
  5.6 170.4 %shard_map.77 = (bf16[16,2048]{1,0:T(8,128)(2,1)S(1)}, f32[1,1]{1,0:T(1,128)}) custom-call(s32[64]{0:T(128)S(1)} %copy-done.2, s32[64]{0:T(128)S(1)} %copy-done.3, bf16[2,128,2304]{2,1,0:T(8,128)(2,1)S(1)} %bitcast.1, bf16[16,2048]{1,0:T(8,128)(2,1)S(1)} %copy-done.1, s32[16,8]{1,0:T(8,128)S(1)} %copy.8.routes_ref, f32[16,8]{1,0:T(8,128)S(1)} %copy.9.gates_ref), custom_call_target="tpu_custom_call" | custom-call | tf_op jit(solution)/shard_map/pallas_call | solution.py:304
  176.0 0.6 copy.12
Async XLA Ops:
  2.1 1.3 copy-start
  3.4 0.8 copy-start.1
  4.3 0.7 copy-start.2
  4.9 0.7 copy-start.3

commit v2 on v1

v2 whole, which is shorter than its diff:
```python
import functools

import jax
import jax.numpy as jnp
from jax import lax
from jax.experimental import pallas as pl
from jax.experimental.pallas import tpu as pltpu
from jax.sharding import PartitionSpec as P

MESH = pl.DeviceIdType.MESH
NX, NY, NZ = 4, 4, 16
ZLO = 8
D = 2048
FF = 768
HALF = FF // 2
ROWS = 16
TOP = 8
CAP = 4
PIECE = 128
COL = NZ * ROWS
SEND = NZ * CAP
CHUNKS = 4
WIDTH = D // CHUNKS
PART = PIECE // CHUNKS
STEPS = NZ // 2
BF16, F32 = jnp.bfloat16, jnp.float32
META = 128
ORDER = (
    "t0", "c0", "s0", "s1", "s2", "t1", "t2", "c1", "t3", "r0", "t4",
    "C0", "C1", "d", "r1", "C2", "C3", "w", "h", "a",
)
STRIDE = 2


def device(x, y, z, core):
    return (x * 2 + z // ZLO, (y * ZLO + z % ZLO) * 2 + core)


def layer_kernel(
    place_any, engine_any, weights, tokens_ref, routes_any, gates_any,
    mixed_ref, load_ref,
    matrix, down_all, token_all, rows_out, rows_all, pick_hi, pick_lo, hidden,
    cross_out, cross_in, own_sum, back_out, back_in, mixing, ring_out, ring_in, final,
    hist_out, hist_in, place_ref, engine_ref, routes_ref, gates_ref,
    local_sem, send_sem, matrix_sem, token_sem, rows_sem, twin_sem,
    cross_sem, back_sem, ring_sem, hist_sem,
):
    dp, ep = lax.axis_index("dp"), lax.axis_index("ep")
    x, z_hi = dp // 2, dp % 2
    y, z_lo, core = ep // 16, (ep // 2) % ZLO, ep % 2
    z = z_hi * ZLO + z_lo
    far = (z + ZLO) % NZ
    z_other = 1 - z_hi
    twin = 1 - core

    fetches = [
        pltpu.make_async_copy(src, dst, local_sem.at[3 + index])
        for index, (src, dst) in enumerate((
            (routes_any, routes_ref), (gates_any, gates_ref), (tokens_ref, token_all.at[z, :, pl.ds(0, D)]),
            (place_any, place_ref), (engine_any, engine_ref)))
    ]
    for copy in fetches:
        copy.start()
    partners = []
    for k in range(NX):
        for other in (core, twin):
            if not (k == 0 and other is core):
                partners.append(device((x + k) % NX, y, z, other))
    for k in range(1, NY):
        for other in (core, twin):
            partners.append(device(x, (y + k) % NY, z, other))
    for other in (core, twin):
        partners.append(device(x, y, far, other))
    along = {step: device(x, y, (z + NZ + step) % NZ, core) for step in (1, 2, -1, -2)}
    partners += list(along.values())
    barrier = pltpu.get_barrier_semaphore()
    for partner in partners:
        pl.semaphore_signal(barrier, inc=1, device_id=partner, device_id_type=MESH)
    for copy in fetches:
        copy.wait()
    gate_parts, rest = [], gates_ref[...]
    for _ in range(3):
        gate_parts.append(rest.astype(BF16).astype(F32))
        rest = rest - gate_parts[-1]
    facts = jnp.concatenate([routes_ref[...].astype(F32)] + gate_parts, axis=0)
    facts = jnp.concatenate([facts, jnp.zeros((4 * TOP, META - ROWS), F32)], axis=1)
    facts = jnp.concatenate([facts, jnp.zeros((META - 4 * TOP, META), F32)], axis=0)
    token_all[z, :, D:] = facts.T[0:ROWS].astype(BF16)
    pl.semaphore_wait(barrier, len(partners))

    sends, waited = [], []

    def send(src, dst, sem, to):
        copy = pltpu.make_async_remote_copy(
            src_ref=src, dst_ref=dst, send_sem=send_sem.at[len(sends)], recv_sem=sem,
            device_id=to, device_id_type=MESH,
        )
        copy.start()
        sends.append(copy)
        return copy

    def arrived(ref, sem):
        pltpu.make_async_copy(ref, ref, sem).wait()

    def piece(part, core_of, dp_of, first=0, count=CHUNKS):
        source = core_of * 8 + dp_of
        if part < 2:
            return matrix.at[part, source, pl.ds(first, count)]
        return down_all.at[pl.ds(first, count), source]

    def piece_sem(part, core_of, dp_of, first=0, count=CHUNKS):
        return matrix_sem.at[part, core_of * 8 + dp_of, first]

    def own_piece(slot, part, half, first=0, count=CHUNKS):
        columns = pl.ds(pl.multiple_of(part * FF + half * HALF, 128), HALF)
        return weights.at[slot, pl.ds(first, count), :, columns]

    def piece_arrived(*at):
        arrived(piece(*at), piece_sem(*at))

    crossing = {}

    def crossed(part, *chunks):
        for copy in crossing.pop((part,) + chunks):
            copy.wait_send()
            waited.append(copy)

    def cross_part(part, *chunks):
        crossing[(part,) + chunks] = []
        for half in (core, twin):
            crossing[(part,) + chunks].append(send(own_piece(z_other, part, half, *chunks), piece(part, core, dp, *chunks),
                 piece_sem(part, core, dp, *chunks), device(x, y, far, half)))

    locals_ = {}

    def spread_part(part):
        locals_[part] = pltpu.make_async_copy(
            own_piece(z_hi, part, core), piece(part, core, dp), local_sem.at[part])
        locals_[part].start()
        for half in (core, twin):
            for k in (1, 3, 2, 0):
                if k == 0 and half is core:
                    continue
                send(own_piece(z_hi, part, half), piece(part, core, dp),
                     piece_sem(part, core, dp), device((x + k) % NX, y, z, half))

    relayed = {0: [], 1: [], 2: []}

    def relay_part(part, *chunks):
        dp_far = x * 2 + z_other
        relayed[part].append(chunks)
        for core_of in (core, twin):
            piece_arrived(part, core_of, dp_far, *chunks)
            for k in (2, 1, 3):
                send(piece(part, core_of, dp_far, *chunks), piece(part, core_of, dp_far, *chunks),
                     piece_sem(part, core_of, dp_far, *chunks), device((x + k) % NX, y, z, core))

    def spread_arrived(part):
        locals_[part].wait()
        for k in range(NX):
            for core_of in (core, twin):
                if not (k == 0 and core_of is core):
                    piece_arrived(part, core_of, ((x + k) % NX) * 2 + z_hi)

    def relay_arrived(part, *chunks):
        for k in range(1, NX):
            for core_of in (core, twin):
                piece_arrived(part, core_of, ((x + k) % NX) * 2 + z_other, *chunks)

    def token_view(block, distance, way):
        if distance == STEPS:
            return token_all.at[block, :, pl.ds((1 - way) * (D // 2), D // 2 + (1 - way) * META)]
        return token_all.at[block]

    def token_send(group, way):
        sign = 1 - 2 * way
        block = (z + NZ - sign * STRIDE * group) % NZ
        for hop in range(STRIDE, 0, -1):
            distance = STRIDE * group + hop
            send(token_view(block, distance, way), token_view(block, distance, way),
                 token_sem.at[way, distance - 1], along[sign * hop])

    def token_group(group):
        for way in range(2):
            if group == 0:
                token_send(0, way)
                continue
            sign = 1 - 2 * way
            block = (z + NZ - sign * STRIDE * group) % NZ
            arrived(token_view(block, STRIDE * group, way), token_sem.at[way, STRIDE * group - 1])
            if group < STEPS // STRIDE:
                token_send(group, way)
        if group == STEPS // STRIDE:
            for way in range(2):
                for distance in [at for at in range(1, STEPS) if at % STRIDE]:
                    block = (z + NZ - (1 - 2 * way) * distance) % NZ
                    arrived(token_view(block, distance, way), token_sem.at[way, distance - 1])

    def dispatch():
        turned = token_all[:, :, D:].reshape(COL, META).astype(F32).T
        chosen = turned[0:TOP]
        gate = turned[TOP:2 * TOP] + turned[2 * TOP:3 * TOP] + turned[3 * TOP:4 * TOP]
        lane64 = lax.broadcasted_iota(jnp.int32, (64, COL), 1)
        row8 = lax.broadcasted_iota(jnp.int32, (8, COL), 0)
        match = jnp.zeros((8, COL), F32)
        hits, weight = [], []
        for k in range(NY):
            wanted = place_ref[2 * (((y + k) % NY) * ZLO + z_lo) + z_hi].astype(F32)
            same = jnp.where(chosen == wanted, 1.0, 0.0)
            hits.append(jnp.sum(same, axis=0, keepdims=True))
            weight.append(jnp.sum(same * gate, axis=0, keepdims=True))
            match = match + jnp.where(row8 == k, hits[k], 0.0)
        before = lax.broadcasted_iota(jnp.int32, (COL, COL), 0)
        after = lax.broadcasted_iota(jnp.int32, (COL, COL), 1)
        earlier = jnp.where((before < after) & (before // ROWS == after // ROWS), 1.0, 0.0).astype(BF16)
        rank = jnp.dot(match.astype(BF16), earlier, preferred_element_type=F32)
        sent_row = lax.broadcasted_iota(jnp.int32, (SEND, COL), 0)
        sent_rank = (sent_row % CAP).astype(F32)
        same_block = sent_row // CAP == lane64 // ROWS
        picks = []
        for k in range(NY):
            picks.append(jnp.where(same_block & (sent_rank == rank[k:k + 1]), hits[k], 0.0))
        pick = jnp.concatenate(picks, axis=0)
        scaled = jnp.concatenate([picks[k] * weight[k] for k in range(NY)], axis=0).T
        high = scaled.astype(BF16)
        pick_hi[...] = high
        pick_lo[...] = (scaled - high.astype(F32)).astype(BF16)
        pick = pick.astype(BF16)
        every = token_all[:, :, 0:D].reshape(COL, D)
        for k in (2, 1, 3, 0):
            moved = jnp.dot(pick[k * SEND:(k + 1) * SEND], every, preferred_element_type=F32).astype(BF16)
            if k == 0:
                rows_all[core, y] = moved
                send(rows_all.at[core, y], rows_all.at[core, y], twin_sem.at[0], device(x, y, z, twin))
            else:
                rows_out[k - 1] = moved
                send(rows_out.at[k - 1], rows_all.at[core, y], rows_sem.at[k], device(x, (y + k) % NY, z, core))

    def count():
        chosen = token_all[:, :, D:].reshape(COL, META).astype(F32).T[0:TOP]
        expert_row = lax.broadcasted_iota(jnp.int32, (64, COL), 0).astype(F32)
        named = jnp.zeros((64, COL), F32)
        for k in range(TOP):
            named = named + jnp.where(chosen[k:k + 1] == expert_row, 1.0, 0.0)
        ours = jnp.where(
            lax.broadcasted_iota(jnp.int32, (8, COL), 1) // (COL // 2) == z_hi, 1.0, 0.0)
        hist_out[...] = lax.dot_general(
            ours, jnp.concatenate([named, jnp.zeros((64, COL), F32)], axis=0),
            (((1,), (1,)), ((), ())), preferred_element_type=F32)
        hist_in[0] = hist_out[...]
        for k in range(NY):
            for index, other in enumerate((core, twin)):
                if k + index > 0:
                    send(hist_out, hist_in.at[2 * k + index], hist_sem.at[2 * k + index],
                         device(x, (y + k) % NY, z, other))

    def exchange_rows():
        for k in (1, 3, 2):
            giver = (y + NY - k) % NY
            arrived(rows_all.at[core, giver], rows_sem.at[k])
            send(rows_all.at[core, giver], rows_all.at[core, giver], twin_sem.at[k], device(x, y, z, twin))
        for k in range(NY):
            arrived(rows_all.at[twin, (y + NY - k) % NY], twin_sem.at[k])

    def first_products():
        for part in range(2):
            spread_arrived(part)
            for chunks in relayed[part]:
                relay_arrived(part, *chunks)
        for plane in range(2):
            rows = rows_all[plane].reshape(NY * SEND, D)
            a = jnp.dot(rows, matrix[0].reshape(D, HALF), preferred_element_type=F32)
            b = jnp.dot(rows, matrix[1].reshape(D, HALF), preferred_element_type=F32)
            hidden[plane] = (a / (1.0 + jnp.exp(-a)) * b).astype(BF16)

    nt = (((1,), (1,)), ((), ()))

    def down_products(chunk):
        if chunk == 0:
            spread_arrived(2)
        relay_arrived(2, chunk, 1)
        down = down_all[chunk].reshape(WIDTH, HALF)
        cross_out[chunk] = lax.dot_general(hidden[twin], down, nt, preferred_element_type=F32).astype(BF16)
        send(cross_out.at[chunk], cross_in.at[chunk], cross_sem.at[chunk], device(x, y, z, twin))
        own_sum[chunk] = lax.dot_general(hidden[core], down, nt, preferred_element_type=F32)

    def rows_back(chunk):
        arrived(cross_in.at[chunk], cross_sem.at[chunk])
        total = (own_sum[chunk] + cross_in[chunk].astype(F32)).astype(BF16)
        back_out[chunk] = total.reshape(NY, SEND, WIDTH)
        for k in (2, 1, 3):
            giver = (y + NY - k) % NY
            send(back_out.at[chunk, giver], back_in.at[chunk, k], back_sem.at[chunk, k], device(x, giver, z, core))
        back_in[chunk, 0] = back_out[chunk, y]

    def reach(chunk, way):
        return STEPS if chunk % 2 == way else STEPS - 2

    def block_of(way, distance):
        return (z + NZ + (1 - 2 * way) * distance) % NZ

    def ring_send(chunk, way, distance):
        hop = 2 - distance % 2
        send(ring_out.at[way, distance - 1, chunk], ring_in.at[way, distance - 1, chunk],
             ring_sem.at[way, distance - 1, chunk], along[(1 - 2 * way) * hop])

    def ring_sum(chunk, way, distance):
        total = mixing[chunk, block_of(way, distance)] if distance else 0.0
        for farther in (distance + 1, distance + 2):
            if farther <= max(reach(chunk, way), STEPS - 1):
                arrived(ring_in.at[way, farther - 1, chunk], ring_sem.at[way, farther - 1, chunk])
                total = total + ring_in[way, farther - 1, chunk].astype(F32)
        return total

    def mix(chunk):
        for k in (1, 3, 2):
            arrived(back_in.at[chunk, k], back_sem.at[chunk, k])
        got = back_in[chunk].reshape(NY * SEND, WIDTH)
        total = jnp.dot(pick_hi[...], got, preferred_element_type=F32)
        total = total + jnp.dot(pick_lo[...], got, preferred_element_type=F32)
        mixing[chunk] = total.reshape(NZ, ROWS, WIDTH)
        for distance in (8, 7, 5, 3, 1):
            for way in range(2):
                if distance <= reach(chunk, way) or distance % 2:
                    ring_out[way, distance - 1, chunk] = mixing[chunk, block_of(way, distance)].astype(BF16)
                    ring_send(chunk, way, distance)

    def ring_step(chunk, distance):
        for way in (chunk % 2, 1 - chunk % 2):
            ring_out[way, distance - 1, chunk] = ring_sum(chunk, way, distance).astype(BF16)
            ring_send(chunk, way, distance)

    def finish(chunk):
        total = mixing[chunk, z] + ring_sum(chunk, 0, 0) + ring_sum(chunk, 1, 0)
        lane = lax.broadcasted_iota(jnp.int32, (ROWS, PIECE), 1)
        for p in range(D // PIECE):
            first = p // CHUNKS * PIECE
            moved = total[:, first:first + PIECE]
            shift = (chunk - p % CHUNKS) % CHUNKS * PART
            if shift:
                moved = pltpu.roll(moved, shift, 1)
            at = pl.ds(p * PIECE, PIECE)
            if chunk == 0:
                final[:, at] = moved
            elif chunk < CHUNKS - 1:
                final[:, at] = jnp.where(lane // PART == chunk, moved, final[:, at])
            else:
                mixed_ref[:, at] = jnp.where(lane // PART == chunk, moved, final[:, at]).astype(BF16)

    stages = {
        "p": crossed, "d": dispatch, "w": exchange_rows, "a": first_products, "h": count,
        "t": token_group, "c": cross_part, "s": spread_part, "r": relay_part,
        "C": lambda chunk: cross_part(2, chunk, 1), "R": lambda chunk: relay_part(2, chunk, 1),
        "Y": down_products, "b": rows_back, "m": mix, "f": finish,
        "x": lambda chunk: ring_step(chunk, 6), "y": lambda chunk: ring_step(chunk, 4),
        "z": lambda chunk: ring_step(chunk, 2),
    }
    for event in ORDER:
        stages[event[0]](*[int(digit) for digit in event[1:]])
    for slot in range(CHUNKS + 7):
        for late, name in enumerate("RYbmxyzf"):
            if 0 <= slot - late < CHUNKS and name + str(slot - late) not in ORDER:
                stages[name](slot - late)

    for index in range(1, 2 * NY):
        arrived(hist_in.at[index], hist_sem.at[index])
    counts = jnp.sum(hist_in[...], axis=0)
    lane = lax.broadcasted_iota(jnp.int32, (8, 128), 1)
    mine = jnp.sum(jnp.where(lane == engine_ref[ep], counts, 0.0), axis=1, keepdims=True)
    load_ref[...] = mine[0:1] / (ROWS * TOP)
    for copy in sends:
        if not any(copy is other for other in waited):
            copy.wait_send()


def on_device(trainer_weights, trainer_place, engine_place, tokens, routes, gates):
    vmem = pl.BlockSpec(memory_space=pltpu.VMEM)
    dma = pltpu.SemaphoreType.DMA
    return pl.pallas_call(
        layer_kernel,
        out_shape=(
            jax.ShapeDtypeStruct((ROWS, D), BF16),
            jax.ShapeDtypeStruct((1, 1), F32),
        ),
        in_specs=[pl.BlockSpec(memory_space=pl.ANY)] * 6,
        out_specs=(vmem, vmem),
        scratch_shapes=[
            pltpu.VMEM((2, 16, CHUNKS, PART, HALF), BF16),
            pltpu.VMEM((CHUNKS, 16, PART, HALF), BF16),
            pltpu.VMEM((NZ, ROWS, D + META), BF16),
            pltpu.VMEM((NY - 1, SEND, D), BF16),
            pltpu.VMEM((2, NY, SEND, D), BF16),
            pltpu.VMEM((COL, NY * SEND), BF16),
            pltpu.VMEM((COL, NY * SEND), BF16),
            pltpu.VMEM((2, NY * SEND, HALF), BF16),
            pltpu.VMEM((CHUNKS, NY * SEND, WIDTH), BF16),
            pltpu.VMEM((CHUNKS, NY * SEND, WIDTH), BF16),
            pltpu.VMEM((CHUNKS, NY * SEND, WIDTH), F32),
            pltpu.VMEM((CHUNKS, NY, SEND, WIDTH), BF16),
            pltpu.VMEM((CHUNKS, NY, SEND, WIDTH), BF16),
            pltpu.VMEM((CHUNKS, NZ, ROWS, WIDTH), F32),
            pltpu.VMEM((2, STEPS, CHUNKS, ROWS, WIDTH), BF16),
            pltpu.VMEM((2, STEPS, CHUNKS, ROWS, WIDTH), BF16),
            pltpu.VMEM((ROWS, D), F32),
            pltpu.VMEM((8, 128), F32),
            pltpu.VMEM((2 * NY, 8, 128), F32),
            pltpu.SMEM((NZ * NY,), jnp.int32),
            pltpu.SMEM((NZ * NY,), jnp.int32),
            pltpu.VMEM((TOP, ROWS), jnp.int32),
            pltpu.VMEM((TOP, ROWS), F32),
            dma((8,)),
            dma((192,)),
            dma((3, 16, CHUNKS)),
            dma((2, STEPS)),
            dma((NY,)),
            dma((NY,)),
            dma((CHUNKS,)),
            dma((CHUNKS, NY)),
            dma((2, STEPS, CHUNKS)),
            dma((2 * NY,)),
        ],
        compiler_params=pltpu.CompilerParams(
            collective_id=0, has_side_effects=True, vmem_limit_bytes=60 * 2**20
        ),
    )(trainer_place, engine_place, trainer_weights[0].reshape(2, CHUNKS, PART, 3 * FF), tokens, routes.T, gates.T)


def solution(mesh):
    in_specs = (
        P("ep", None, "dp", None),
        P(),
        P(),
        P(("dp", "ep"), None),
        P(("dp", "ep"), None),
        P(("dp", "ep"), None),
    )
    out_specs = (P(("dp", "ep"), None), P("dp", "ep"))
    return jax.shard_map(
        on_device, mesh=mesh, in_specs=in_specs, out_specs=out_specs, check_vma=False
    )
```

time: 179 us -> 136 us (0.76)
  the two profiles are of different devices: /device:TPU:32 before, /device:TPU:1 now
where the time goes in v2:
time: 136 us; the launch traced here: 134 us
  Pallas kernels  131 us (96%)
  between operations  2.39 us (2%)
  local copies, waits for them, and re-layouts  1.47 us (1%)
    pallas_call x1, Pallas kernels, on_device(): pl.pallas_call(layer_kernel, out_shape=(jax.ShapeDtypeStruct((ROWS, D), B...  131 us

profile of v2, /device:TPU:1, one launch (start us, length us, event | category | flops | bytes accessed | tf_op | source)
XLA Modules:
  0.0 134.4 jit_solution(14366541817831842600)
XLA Ops:
  0.6 130.5 %shard_map.77 = (bf16[16,2048]{1,0:T(8,128)(2,1)}, f32[1,1]{1,0:T(1,128)}) custom-call(s32[64]{0:T(128)} %place_any.1, s32[64]{0:T(128)} %engine_any.1, bf16[2,4,32,2304]{3,2,1,0:T(8,128)(2,1)} %bitcast.3, bf16[16,2048]{1,0:T(8,128)(2,1)} %tokens_ref.1, s32[8,16]{1,0:T(8,128)} %bitcast.4, f32[8,16]{1,0:T(8,128)} %bitcast.5), custom_call_target="tpu_custom_call" | custom-call | tf_op jit(solution)/shard_map/pallas_call | solution.py:379
  131.2 1.5 %copy.10 = bf16[16,2048]{1,0:T(8,128)(2,1)} copy(bf16[16,2048]{1,0:T(8,128)(2,1)} %get-tuple-element.4) | data formatting | bytes 131072

commit v3 on v2

--- a/solution.py
+++ b/solution.py
@@ -27,9 +27,10 @@
 META = 128
 ORDER = (
     "t0", "c0", "s0", "s1", "s2", "t1", "t2", "c1", "t3", "r0", "t4",
-    "C0", "C1", "d", "r1", "C2", "C3", "w", "h", "a",
+    "d", "r1", "C0", "C1", "C2", "C3", "w", "h", "a",
 )
 STRIDE = 2
+STOPS = ((6, 4, 2, 0), (6, 4, 2, 0), (6, 4, 2, 0), (5, 2, 0))
 
 
 def device(x, y, z, core):
@@ -61,7 +62,7 @@
     ]
     for copy in fetches:
         copy.start()
-    partners = []
+    partners = [device(x, y, far, other) for other in (core, twin)]
     for k in range(NX):
         for other in (core, twin):
             if not (k == 0 and other is core):
@@ -69,9 +70,7 @@
     for k in range(1, NY):
         for other in (core, twin):
             partners.append(device(x, (y + k) % NY, z, other))
-    for other in (core, twin):
-        partners.append(device(x, y, far, other))
-    along = {step: device(x, y, (z + NZ + step) % NZ, core) for step in (1, 2, -1, -2)}
+    along = {step: device(x, y, (z + NZ + step) % NZ, core) for step in (1, 2, 3, -1, -2, -3)}
     partners += list(along.values())
     barrier = pltpu.get_barrier_semaphore()
     for partner in partners:
@@ -293,21 +292,24 @@
             send(back_out.at[chunk, giver], back_in.at[chunk, k], back_sem.at[chunk, k], device(x, giver, z, core))
         back_in[chunk, 0] = back_out[chunk, y]
 
+    def next_stop(chunk, distance):
+        return max(stop for stop in STOPS[chunk] if stop < distance)
+
     def reach(chunk, way):
-        return STEPS if chunk % 2 == way else STEPS - 2
+        return STEPS if chunk % 2 == way else STEPS - 1
 
     def block_of(way, distance):
         return (z + NZ + (1 - 2 * way) * distance) % NZ
 
     def ring_send(chunk, way, distance):
-        hop = 2 - distance % 2
+        hop = distance - next_stop(chunk, distance)
         send(ring_out.at[way, distance - 1, chunk], ring_in.at[way, distance - 1, chunk],
              ring_sem.at[way, distance - 1, chunk], along[(1 - 2 * way) * hop])
 
     def ring_sum(chunk, way, distance):
         total = mixing[chunk, block_of(way, distance)] if distance else 0.0
-        for farther in (distance + 1, distance + 2):
-            if farther <= max(reach(chunk, way), STEPS - 1):
+        for farther in range(1, reach(chunk, way) + 1):
+            if next_stop(chunk, farther) == distance:
                 arrived(ring_in.at[way, farther - 1, chunk], ring_sem.at[way, farther - 1, chunk])
                 total = total + ring_in[way, farther - 1, chunk].astype(F32)
         return total
@@ -319,13 +321,16 @@
         total = jnp.dot(pick_hi[...], got, preferred_element_type=F32)
         total = total + jnp.dot(pick_lo[...], got, preferred_element_type=F32)
         mixing[chunk] = total.reshape(NZ, ROWS, WIDTH)
-        for distance in (8, 7, 5, 3, 1):
+        for distance in range(STEPS, 0, -1):
             for way in range(2):
-                if distance <= reach(chunk, way) or distance % 2:
+                if distance <= reach(chunk, way) and distance not in STOPS[chunk]:
                     ring_out[way, distance - 1, chunk] = mixing[chunk, block_of(way, distance)].astype(BF16)
                     ring_send(chunk, way, distance)
 
-    def ring_step(chunk, distance):
+    def ring_step(chunk, step):
+        distance = STOPS[chunk][step]
+        if distance == 0:
+            return finish(chunk)
         for way in (chunk % 2, 1 - chunk % 2):
             ring_out[way, distance - 1, chunk] = ring_sum(chunk, way, distance).astype(BF16)
             ring_send(chunk, way, distance)
@@ -351,16 +356,19 @@
         "p": crossed, "d": dispatch, "w": exchange_rows, "a": first_products, "h": count,
         "t": token_group, "c": cross_part, "s": spread_part, "r": relay_part,
         "C": lambda chunk: cross_part(2, chunk, 1), "R": lambda chunk: relay_part(2, chunk, 1),
-        "Y": down_products, "b": rows_back, "m": mix, "f": finish,
-        "x": lambda chunk: ring_step(chunk, 6), "y": lambda chunk: ring_step(chunk, 4),
-        "z": lambda chunk: ring_step(chunk, 2),
+        "Y": down_products, "b": rows_back, "m": mix,
     }
     for event in ORDER:
         stages[event[0]](*[int(digit) for digit in event[1:]])
     for slot in range(CHUNKS + 7):
-        for late, name in enumerate("RYbmxyzf"):
-            if 0 <= slot - late < CHUNKS and name + str(slot - late) not in ORDER:
-                stages[name](slot - late)
+        for late in range(8):
+            chunk = slot - late
+            if 0 <= chunk < CHUNKS:
+                if late < 4:
+                    stages["RYbm"[late]](chunk)
+                elif late - 4 < len(STOPS[chunk]) - (chunk == CHUNKS - 1):
+                    ring_step(chunk, late - 4)
+    finish(CHUNKS - 1)
 
     for index in range(1, 2 * NY):
         arrived(hist_in.at[index], hist_sem.at[index])

time: 136 us -> 134 us (0.985)
  Pallas kernels: 131 us -> 128 us
    pallas_call x1, Pallas kernels: 131 us -> 128 us  [on_device(): pl.pallas_call(layer_kernel, out_shape=(jax.ShapeDtypeStruct((ROWS, D), B...]
where the time goes in v3:
time: 134 us; the launch traced here: 132 us
  Pallas kernels  128 us (96%)
  between operations  2.39 us (2%)
  local copies, waits for them, and re-layouts  1.47 us (1%)
    pallas_call x1, Pallas kernels, on_device(): pl.pallas_call(layer_kernel, out_shape=(jax.ShapeDtypeStruct((ROWS, D), B...  128 us

profile of v3, /device:TPU:1, one launch (start us, length us, event | category | flops | bytes accessed | tf_op | source)
XLA Modules:
  0.0 132.3 jit_solution(2857978727701864256)
XLA Ops:
  0.6 128.5 %shard_map.77 = (bf16[16,2048]{1,0:T(8,128)(2,1)}, f32[1,1]{1,0:T(1,128)}) custom-call(s32[64]{0:T(128)} %place_any.1, s32[64]{0:T(128)} %engine_any.1, bf16[2,4,32,2304]{3,2,1,0:T(8,128)(2,1)} %bitcast.3, bf16[16,2048]{1,0:T(8,128)(2,1)} %tokens_ref.1, s32[8,16]{1,0:T(8,128)} %bitcast.4, f32[8,16]{1,0:T(8,128)} %bitcast.5), custom_call_target="tpu_custom_call" | custom-call | tf_op jit(solution)/shard_map/pallas_call | solution.py:387
  129.1 1.5 %copy.10 = bf16[16,2048]{1,0:T(8,128)(2,1)} copy(bf16[16,2048]{1,0:T(8,128)(2,1)} %get-tuple-element.4) | data formatting | bytes 131072

commit v4 on v3

--- a/solution.py
+++ b/solution.py
@@ -27,7 +27,7 @@
 META = 128
 ORDER = (
     "t0", "c0", "s0", "s1", "s2", "t1", "t2", "c1", "t3", "r0", "t4",
-    "d", "r1", "C0", "C1", "C2", "C3", "w", "h", "a",
+    "d", "r1", "C0", "C1", "C2", "C3", "w", "a", "h",
 )
 STRIDE = 2
 STOPS = ((6, 4, 2, 0), (6, 4, 2, 0), (6, 4, 2, 0), (5, 2, 0))
@@ -220,10 +220,6 @@
         for k in range(NY):
             picks.append(jnp.where(same_block & (sent_rank == rank[k:k + 1]), hits[k], 0.0))
         pick = jnp.concatenate(picks, axis=0)
-        scaled = jnp.concatenate([picks[k] * weight[k] for k in range(NY)], axis=0).T
-        high = scaled.astype(BF16)
-        pick_hi[...] = high
-        pick_lo[...] = (scaled - high.astype(F32)).astype(BF16)
         pick = pick.astype(BF16)
         every = token_all[:, :, 0:D].reshape(COL, D)
         for k in (2, 1, 3, 0):
@@ -234,6 +230,10 @@
             else:
                 rows_out[k - 1] = moved
                 send(rows_out.at[k - 1], rows_all.at[core, y], rows_sem.at[k], device(x, (y + k) % NY, z, core))
+        scaled = jnp.concatenate([picks[k] * weight[k] for k in range(NY)], axis=0).T
+        high = scaled.astype(BF16)
+        pick_hi[...] = high
+        pick_lo[...] = (scaled - high.astype(F32)).astype(BF16)
 
     def count():
         chosen = token_all[:, :, D:].reshape(COL, META).astype(F32).T[0:TOP]

time: 134 us -> 134 us (level)
  no operation moved by 1% of the time
where the time goes in v4:
time: 134 us; the launch traced here: 132 us
  Pallas kernels  128 us (96%)
  between operations  2.39 us (2%)
  local copies, waits for them, and re-layouts  1.47 us (1%)
    pallas_call x1, Pallas kernels, on_device(): pl.pallas_call(layer_kernel, out_shape=(jax.ShapeDtypeStruct((ROWS, D), B...  128 us

profile of v4, /device:TPU:1, one launch (start us, length us, event | category | flops | bytes accessed | tf_op | source)
XLA Modules:
  0.0 131.9 jit_solution(16102630186293337703)
XLA Ops:
  0.6 128.0 %shard_map.77 = (bf16[16,2048]{1,0:T(8,128)(2,1)}, f32[1,1]{1,0:T(1,128)}) custom-call(s32[64]{0:T(128)} %place_any.1, s32[64]{0:T(128)} %engine_any.1, bf16[2,4,32,2304]{3,2,1,0:T(8,128)(2,1)} %bitcast.3, bf16[16,2048]{1,0:T(8,128)(2,1)} %tokens_ref.1, s32[8,16]{1,0:T(8,128)} %bitcast.4, f32[8,16]{1,0:T(8,128)} %bitcast.5), custom_call_target="tpu_custom_call" | custom-call | tf_op jit(solution)/shard_map/pallas_call | solution.py:387
  128.7 1.5 %copy.10 = bf16[16,2048]{1,0:T(8,128)(2,1)} copy(bf16[16,2048]{1,0:T(8,128)(2,1)} %get-tuple-element.4) | data formatting | bytes 131072
